TPU v7x, 512 devices: a whole 4x8x8 slice. The times are simulated.
512 devices in a mesh: dp: 4 (over x), row: 16 (over y, core), col: 8 (over z).
Axes of the slice: x: 4, y: 8, z: 8, core: 2. Of those that a mesh axis runs over, the one named last changes fastest.
Arguments:
- grad_wi: bfloat16 [4, 4096, 16384], P('dp', 'row', 'col'), may hold values from -100 to 100
- grad_wo: bfloat16 [4, 16384, 4096], P('dp', 'row', 'col'), may hold values from -100 to 100
- row_wi: float32 [4096], P('row'), may hold values from 0.01 to 1
- col_wi: float32 [16384], P('col'), may hold values from 0.01 to 1
- row_wo: float32 [16384], P('row'), may hold values from 0.01 to 1
- col_wo: float32 [4096], P('col'), may hold values from 0.01 to 1
Outputs:
- update_wi: bfloat16 [4096, 16384], P('row', 'col')
- row_wi_new: float32 [4096], P('row')
- col_wi_new: float32 [16384], P('col')
- update_wo: bfloat16 [16384, 4096], P('row', 'col')
- row_wo_new: float32 [16384], P('row')
- col_wo_new: float32 [4096], P('col')
All inputs are finite; a program needn't handle non-finite values.
Results may differ from a plain program's by a relative error of at most 0.015.
Values may be sent and summed in bfloat16 or wider, within the bound.
A program may use at most 64 MiB of HBM per device.

v0:
```python
import jax
import jax.numpy as jnp
from jax import lax
from jax.sharding import PartitionSpec as P

D = 4096
FF = 16384
BETA = 0.8
EPS_SQUARE = 1e-30


def column_totals(square_wi, square_wo):
    return lax.psum((jnp.sum(square_wi, axis=0), jnp.sum(square_wo, axis=0)), "row")


def local(grad_wi, grad_wo, row_wi, col_wi, row_wo, col_wo):
    terms = (grad_wi[0].astype(jnp.float32), grad_wo[0].astype(jnp.float32))
    total_wi, total_wo = (
        lax.psum(terms[0].astype(jnp.bfloat16), "dp").astype(jnp.float32),
        lax.psum(terms[1].astype(jnp.bfloat16), "dp").astype(jnp.float32),
    )
    square_wi = total_wi * total_wi + EPS_SQUARE
    square_wo = total_wo * total_wo + EPS_SQUARE
    row_sum_wi, row_sum_wo = lax.psum(
        (jnp.sum(square_wi, axis=1), jnp.sum(square_wo, axis=1)), "col"
    )
    col_sum_wi, col_sum_wo = column_totals(square_wi, square_wo)
    row_new_wi = BETA * row_wi + (1.0 - BETA) * (row_sum_wi / FF)
    row_new_wo = BETA * row_wo + (1.0 - BETA) * (row_sum_wo / D)
    col_new_wi = BETA * col_wi + (1.0 - BETA) * (col_sum_wi / D)
    col_new_wo = BETA * col_wo + (1.0 - BETA) * (col_sum_wo / FF)
    raw_wi = total_wi / jnp.sqrt(row_new_wi[:, None] * col_new_wi[None, :])
    raw_wo = total_wo / jnp.sqrt(row_new_wo[:, None] * col_new_wo[None, :])
    local_squares = (jnp.sum(raw_wi * raw_wi), jnp.sum(raw_wo * raw_wo))
    energy_wi, energy_wo = lax.psum((local_squares[0], local_squares[1]), ("row", "col"))
    update_wi = (raw_wi / jnp.maximum(1.0, jnp.sqrt(energy_wi / (D * FF)))).astype(jnp.bfloat16)
    update_wo = (raw_wo / jnp.maximum(1.0, jnp.sqrt(energy_wo / (D * FF)))).astype(jnp.bfloat16)
    return (update_wi, row_new_wi, col_new_wi, update_wo, row_new_wo, col_new_wo)


def solution(mesh):
    return jax.shard_map(
        local,
        mesh=mesh,
        in_specs=(
            P("dp", "row", "col"),
            P("dp", "row", "col"),
            P("row"),
            P("col"),
            P("row"),
            P("col"),
        ),
        out_specs=(P("row", "col"), P("row"), P("col"), P("row", "col"), P("row"), P("col")),
        check_vma=False,
    )
```

profile of v0, /device:TPU:64, one launch (start us, length us, event | category | flops | bytes accessed | tf_op | source)
XLA Modules:
  0.0 412.7 jit_solution(8415651941492895730)
XLA Ops:
  7.2 0.0 all-reduce.6.cloned.1.call-start
  7.2 0.7 all-reduce.6.cloned.1.call-update
  7.9 76.1 %all-reduce.6.cloned.1.call-done = (bf16[256,2048]{1,0:T(8,128)(2,1)}, bf16[1024,512]{1,0:T(8,128)(2,1)}) async-done(((bf16[256,2048]{1,0:T(8,128)(2,1)}, bf16[1024,512]{1,0:T(8,128)(2,1)}), (bf16[256,2048]{1,0:T(8,128)(2,1)}, bf16[1024,512]{1,0:T(8,128)(2,1)})) %all-reduce.6.cloned.1.call-update) | async-done | bytes 2097168 | tf_op jit(solution)/shard_map/psum | solution.py:19
  84.0 0.0 copy-start.1
  84.0 0.0 copy-start.9
  84.0 0.0 copy-start.7
  84.0 0.0 copy-start.6
  84.0 1.8 fusion.5
  85.8 0.0 copy-done.1
  85.8 0.0 copy-start.8
  85.8 0.0 copy-start
  85.8 0.5 fusion.2
  86.3 16.8 %all-reduce.2 = (f32[256]{0:T(256)S(1)}, f32[1024]{0:T(1024)S(1)}) all-reduce(f32[256]{0:T(256)S(1)} %get-tuple-element.8, f32[1024]{0:T(1024)S(1)} %get-tuple-element.6), channel_id=1, replica_groups=mesh['dp'=4,'row'=16,'col'=8] {'col'}, use_global_device_ids=true, to_apply=%region_2.0 | all-reduce | flops 1280 | bytes 10240 | tf_op jit(solution)/shard_map/psum | solution.py:24
  103.1 0.0 copy-done.9
  103.1 0.0 copy-start.5
  103.1 0.0 copy-done.7
  103.1 0.0 copy-start.3
  103.2 45.7 %all-reduce.1 = (f32[2048]{0:T(1024)S(1)}, f32[512]{0:T(512)S(1)}) all-reduce(f32[2048]{0:T(1024)S(1)} %get-tuple-element.9, f32[512]{0:T(512)S(1)} %get-tuple-element.7), channel_id=1, replica_groups=mesh['dp'=4,'row'=16,'col'=8] {'row'}, use_global_device_ids=true, to_apply=%region_4.0 | all-reduce | flops 2560 | bytes 20480 | tf_op jit(solution)/shard_map/psum | solution.py:13
  148.9 0.0 copy-done.6
  148.9 0.0 copy-start.2
  148.9 1.5 multiply_reduce_fusion.1
  150.4 0.0 copy-done.8
  150.4 0.0 copy-done
  150.4 0.0 copy-start.4
  150.4 1.4 multiply_reduce_fusion
  151.9 249.7 %all-reduce = (f32[]{:T(128)}, f32[]{:T(128)}) all-reduce(f32[]{:T(128)} %multiply_reduce_fusion.1, f32[]{:T(128)} %multiply_reduce_fusion), channel_id=1, replica_groups=mesh['dp'=4,'row'=16,'col'=8] {'row','col'}, use_global_device_ids=true, to_apply=%region_6.0 | all-reduce | flops 2 | bytes 16 | tf_op jit(solution)/shard_map/psum | solution.py:35
  403.0 0.0 copy-done.5
  403.0 0.0 copy-done.2
  403.0 1.4 divide_convert_fusion.1
  404.4 0.0 copy-done.3
  404.4 0.0 copy-done.4
  404.4 1.4 divide_convert_fusion
  (4 shorter events, 0.0 us)
Async XLA Ops:
  7.2 76.8 %all-reduce.6.cloned.1.call-start = ((), (), s32[]{:S(2)}) async-start(), calls=%async_computation | async-start | bytes 4194304 | tf_op jit(solution)/shard_map/psum | solution.py:19
  84.0 1.8 copy-start.1
  84.0 19.1 %copy-start.9 = (f32[256]{0:T(256)S(1)}, f32[256]{0:T(256)}, u32[]{:S(2)}) copy-start(f32[256]{0:T(256)} %param.8) | copy-start | bytes 3076
  84.0 19.1 %copy-start.7 = (f32[1024]{0:T(1024)S(1)}, f32[1024]{0:T(1024)}, u32[]{:S(2)}) copy-start(f32[1024]{0:T(1024)} %param.10) | copy-start | bytes 12292
  84.0 64.9 %copy-start.6 = (f32[2048]{0:T(1024)S(1)}, f32[2048]{0:T(1024)}, u32[]{:S(2)}) copy-start(f32[2048]{0:T(1024)} %param.9) | copy-start | bytes 24580
  85.8 64.6 %copy-start.8 = (f32[512]{0:T(512)S(1)}, f32[512]{0:T(512)}, u32[]{:S(2)}) copy-start(f32[512]{0:T(512)} %param.11) | copy-start | bytes 6148
  85.8 64.6 %copy-start = (bf16[1024,512]{1,0:T(8,128)(2,1)S(1)}, bf16[1024,512]{1,0:T(8,128)(2,1)}, u32[]{:S(2)}) copy-start(bf16[1024,512]{1,0:T(8,128)(2,1)} %get-tuple-element.17) | copy-start | bytes 3145732
  103.1 299.9 %copy-start.5 = (f32[256]{0:T(256)}, f32[256]{0:T(256)S(1)}, u32[]{:S(2)}) copy-start(f32[256]{0:T(256)S(1)} %multiply_add_fusion.3) | copy-start | bytes 3076
  103.1 301.3 %copy-start.3 = (f32[1024]{0:T(1024)}, f32[1024]{0:T(1024)S(1)}, u32[]{:S(2)}) copy-start(f32[1024]{0:T(1024)S(1)} %multiply_add_fusion.1) | copy-start | bytes 12292
  148.9 254.1 %copy-start.2 = (f32[2048]{0:T(1024)}, f32[2048]{0:T(1024)S(1)}, u32[]{:S(2)}) copy-start(f32[2048]{0:T(1024)S(1)} %multiply_add_fusion) | copy-start | bytes 24580
  150.4 254.0 %copy-start.4 = (f32[512]{0:T(512)}, f32[512]{0:T(512)S(1)}, u32[]{:S(2)}) copy-start(f32[512]{0:T(512)S(1)} %multiply_add_fusion.2) | copy-start | bytes 6148
Sparse Core Ops, SparseCore 0:
  10.4 73.4 all-reduce.5
where the time goes:
time: 413 us
  blocking collectives  312 us (76%)
  waiting for transfers between devices  76.8 us (19%)
  between operations  15.5 us (4%)
  other arithmetic  8.11 us (2%)
    psum x1, blocking collectives, local(): lax.psum((local_squares[0], local_squares[1]), ('row', 'col'))  250 us
    psum x1, waiting for transfers between devices, local(): lax.psum(terms[0].astype(jnp.bfloat16), 'dp').astype(jnp.float32)  76.1 us
    psum x1, blocking collectives, column_totals(): lax.psum((jnp.sum(square_wi, axis=0), jnp.sum(square_wo, axis=0)), 'row')  45.7 us
    psum x1, blocking collectives, local(): lax.psum((jnp.sum(square_wi, axis=1), jnp.sum(square_wo, axis=1)), 'col')  16.8 us
  transfers between devices with their start and end apart: 1, of which 1 were waited for; matrix products, arithmetic and copies ran while one was open for 0% of the time, Pallas kernels for 0%

commit v1 on v0

--- a/solution.py
+++ b/solution.py
@@ -32,7 +32,7 @@
     raw_wi = total_wi / jnp.sqrt(row_new_wi[:, None] * col_new_wi[None, :])
     raw_wo = total_wo / jnp.sqrt(row_new_wo[:, None] * col_new_wo[None, :])
     local_squares = (jnp.sum(raw_wi * raw_wi), jnp.sum(raw_wo * raw_wo))
-    energy_wi, energy_wo = lax.psum((local_squares[0], local_squares[1]), ("row", "col"))
+    energy_wi, energy_wo = lax.psum(lax.psum((local_squares[0], local_squares[1]), "col"), "row")
     update_wi = (raw_wi / jnp.maximum(1.0, jnp.sqrt(energy_wi / (D * FF)))).astype(jnp.bfloat16)
     update_wo = (raw_wo / jnp.maximum(1.0, jnp.sqrt(energy_wo / (D * FF)))).astype(jnp.bfloat16)
     return (update_wi, row_new_wi, col_new_wi, update_wo, row_new_wo, col_new_wo)

time: 413 us -> 206 us (0.50)
  the two profiles are of different devices: /device:TPU:64 before, /device:TPU:1 now
where the time goes in v1:
time: 206 us
  blocking collectives  104 us (50%)
  waiting for transfers between devices  78.3 us (38%)
  between operations  15.5 us (8%)
  other arithmetic  8.11 us (4%)
    psum x1, waiting for transfers between devices, local(): lax.psum(terms[0].astype(jnp.bfloat16), 'dp').astype(jnp.float32)  77.6 us
    psum x1, blocking collectives, column_totals(): lax.psum((jnp.sum(square_wi, axis=0), jnp.sum(square_wo, axis=0)), 'row')  46.7 us
    psum x1, blocking collectives, local(): lax.psum(lax.psum((local_squares[0], local_squares[1]), 'col'), 'row')  30.8 us
    psum x1, blocking collectives, local(): lax.psum((jnp.sum(square_wi, axis=1), jnp.sum(square_wo, axis=1)), 'col')  14.6 us
    psum x1, blocking collectives, local(): lax.psum((local_squares[0], local_squares[1]), 'col')  11.6 us
  transfers between devices with their start and end apart: 1, of which 1 were waited for; matrix products, arithmetic and copies ran while one was open for 0% of the time, Pallas kernels for 0%

profile of v1, /device:TPU:1, one launch (start us, length us, event | category | flops | bytes accessed | tf_op | source)
XLA Modules:
  0.0 205.7 jit_solution(5595017636434755267)
XLA Ops:
  7.2 0.0 all-reduce.7.cloned.1.call-start
  7.2 0.7 all-reduce.7.cloned.1.call-update
  7.9 77.6 %all-reduce.7.cloned.1.call-done = (bf16[256,2048]{1,0:T(8,128)(2,1)}, bf16[1024,512]{1,0:T(8,128)(2,1)}) async-done(((bf16[256,2048]{1,0:T(8,128)(2,1)}, bf16[1024,512]{1,0:T(8,128)(2,1)}), (bf16[256,2048]{1,0:T(8,128)(2,1)}, bf16[1024,512]{1,0:T(8,128)(2,1)})) %all-reduce.7.cloned.1.call-update) | async-done | bytes 2097168 | tf_op jit(solution)/shard_map/psum | solution.py:19
  85.5 0.0 copy-start.1
  85.5 0.0 copy-start.9
  85.5 0.0 copy-start.7
  85.5 0.0 copy-start.6
  85.5 1.8 fusion.5
  87.3 0.0 copy-done.1
  87.3 0.0 copy-start.8
  87.3 0.0 copy-start
  87.4 0.5 fusion.2
  87.9 14.6 %all-reduce.3 = (f32[256]{0:T(256)S(1)}, f32[1024]{0:T(1024)S(1)}) all-reduce(f32[256]{0:T(256)S(1)} %get-tuple-element.8, f32[1024]{0:T(1024)S(1)} %get-tuple-element.6), channel_id=1, replica_groups=mesh['dp'=4,'row'=16,'col'=8] {'col'}, use_global_device_ids=true, to_apply=%region_2.0 | all-reduce | flops 1280 | bytes 10240 | tf_op jit(solution)/shard_map/psum | solution.py:24
  102.5 0.0 copy-done.9
  102.5 0.0 copy-start.5
  102.5 0.0 copy-done.7
  102.5 0.0 copy-start.3
  102.5 46.7 %all-reduce.1 = (f32[2048]{0:T(1024)S(1)}, f32[512]{0:T(512)S(1)}) all-reduce(f32[2048]{0:T(1024)S(1)} %get-tuple-element.9, f32[512]{0:T(512)S(1)} %get-tuple-element.7), channel_id=1, replica_groups=mesh['dp'=4,'row'=16,'col'=8] {'row'}, use_global_device_ids=true, to_apply=%region_4.0 | all-reduce | flops 2560 | bytes 20480 | tf_op jit(solution)/shard_map/psum | solution.py:13
  149.2 0.0 copy-done.6
  149.2 0.0 copy-start.2
  149.2 1.5 multiply_reduce_fusion.1
  150.7 0.0 copy-done.8
  150.7 0.0 copy-done
  150.7 0.0 copy-start.4
  150.8 1.4 multiply_reduce_fusion
  152.2 11.6 %all-reduce.2 = (f32[]{:T(128)}, f32[]{:T(128)}) all-reduce(f32[]{:T(128)} %multiply_reduce_fusion.1, f32[]{:T(128)} %multiply_reduce_fusion), channel_id=1, replica_groups=mesh['dp'=4,'row'=16,'col'=8] {'col'}, use_global_device_ids=true, to_apply=%region_6.0 | all-reduce | flops 2 | bytes 16 | tf_op jit(solution)/shard_map/psum | solution.py:35
  163.7 30.8 %all-reduce = (f32[]{:T(128)}, f32[]{:T(128)}) all-reduce(f32[]{:T(128)} %get-tuple-element.14, f32[]{:T(128)} %get-tuple-element.15), channel_id=1, replica_groups=mesh['dp'=4,'row'=16,'col'=8] {'row'}, use_global_device_ids=true, to_apply=%region_7.0 | all-reduce | flops 2 | bytes 16 | tf_op jit(solution)/shard_map/psum | solution.py:35
  195.9 0.0 copy-done.5
  196.0 0.0 copy-done.2
  196.0 1.4 divide_convert_fusion.1
  197.4 0.0 copy-done.3
  197.4 0.0 copy-done.4
  197.4 1.4 divide_convert_fusion
  (4 shorter events, 0.0 us)
Async XLA Ops:
  7.2 78.4 %all-reduce.7.cloned.1.call-start = ((), (), s32[]{:S(2)}) async-start(), calls=%async_computation | async-start | bytes 4194304 | tf_op jit(solution)/shard_map/psum | solution.py:19
  85.5 1.8 copy-start.1
  85.5 16.9 %copy-start.9 = (f32[256]{0:T(256)S(1)}, f32[256]{0:T(256)}, u32[]{:S(2)}) copy-start(f32[256]{0:T(256)} %param.8) | copy-start | bytes 3076
  85.5 17.0 %copy-start.7 = (f32[1024]{0:T(1024)S(1)}, f32[1024]{0:T(1024)}, u32[]{:S(2)}) copy-start(f32[1024]{0:T(1024)} %param.10) | copy-start | bytes 12292
  85.5 63.7 %copy-start.6 = (f32[2048]{0:T(1024)S(1)}, f32[2048]{0:T(1024)}, u32[]{:S(2)}) copy-start(f32[2048]{0:T(1024)} %param.9) | copy-start | bytes 24580
  87.3 63.4 %copy-start.8 = (f32[512]{0:T(512)S(1)}, f32[512]{0:T(512)}, u32[]{:S(2)}) copy-start(f32[512]{0:T(512)} %param.11) | copy-start | bytes 6148
  87.3 63.4 %copy-start = (bf16[1024,512]{1,0:T(8,128)(2,1)S(1)}, bf16[1024,512]{1,0:T(8,128)(2,1)}, u32[]{:S(2)}) copy-start(bf16[1024,512]{1,0:T(8,128)(2,1)} %get-tuple-element.19) | copy-start | bytes 3145732
  102.5 93.5 %copy-start.5 = (f32[256]{0:T(256)}, f32[256]{0:T(256)S(1)}, u32[]{:S(2)}) copy-start(f32[256]{0:T(256)S(1)} %multiply_add_fusion.3) | copy-start | bytes 3076
  102.5 94.9 %copy-start.3 = (f32[1024]{0:T(1024)}, f32[1024]{0:T(1024)S(1)}, u32[]{:S(2)}) copy-start(f32[1024]{0:T(1024)S(1)} %multiply_add_fusion.1) | copy-start | bytes 12292
  149.2 46.8 %copy-start.2 = (f32[2048]{0:T(1024)}, f32[2048]{0:T(1024)S(1)}, u32[]{:S(2)}) copy-start(f32[2048]{0:T(1024)S(1)} %multiply_add_fusion) | copy-start | bytes 24580
  150.7 46.6 %copy-start.4 = (f32[512]{0:T(512)}, f32[512]{0:T(512)S(1)}, u32[]{:S(2)}) copy-start(f32[512]{0:T(512)S(1)} %multiply_add_fusion.2) | copy-start | bytes 6148
Sparse Core Ops, SparseCore 0:
  10.4 75.0 all-reduce.6

commit v2 on v0

--- a/solution.py
+++ b/solution.py
@@ -16,7 +16,7 @@
 def local(grad_wi, grad_wo, row_wi, col_wi, row_wo, col_wo):
     terms = (grad_wi[0].astype(jnp.float32), grad_wo[0].astype(jnp.float32))
     total_wi, total_wo = (
-        lax.psum(terms[0].astype(jnp.bfloat16), "dp").astype(jnp.float32),
+        jnp.sum(lax.all_gather(terms[0].astype(jnp.bfloat16), "dp"), axis=0).astype(jnp.float32),
         lax.psum(terms[1].astype(jnp.bfloat16), "dp").astype(jnp.float32),
     )
     square_wi = total_wi * total_wi + EPS_SQUARE

time: 413 us -> 458 us (1.11)
  waiting for transfers between devices: 76.8 us -> 119 us
    all_gather x0 -> x1, waiting for transfers between devices: none -> 55.1 us  [local(): lax.all_gather(terms[0].astype(jnp.bfloat16), 'dp')]
    psum x1, waiting for transfers between devices: 76.1 us -> 62.2 us  [local(): lax.psum(terms[1].astype(jnp.bfloat16), 'dp').astype(jnp.float32)]
  transfers between devices with their start and end apart: 1 -> 2, of which waited for: 1 -> 2; matrix products, arithmetic and copies ran while one was open for 0% -> 0% of each run, Pallas kernels for 0% -> 0%
where the time goes in v2:
time: 458 us
  blocking collectives  312 us (68%)
  waiting for transfers between devices  119 us (26%)
  between operations  15.5 us (3%)
  other arithmetic  11.1 us (2%)
    psum x1, blocking collectives, local(): lax.psum((local_squares[0], local_squares[1]), ('row', 'col'))  250 us
    psum x1, waiting for transfers between devices, local(): lax.psum(terms[1].astype(jnp.bfloat16), 'dp').astype(jnp.float32)  62.2 us
    all_gather x1, waiting for transfers between devices, local(): lax.all_gather(terms[0].astype(jnp.bfloat16), 'dp')  55.1 us
    psum x1, blocking collectives, column_totals(): lax.psum((jnp.sum(square_wi, axis=0), jnp.sum(square_wo, axis=0)), 'row')  45.7 us
    psum x1, blocking collectives, local(): lax.psum((jnp.sum(square_wi, axis=1), jnp.sum(square_wo, axis=1)), 'col')  16.8 us
  transfers between devices with their start and end apart: 2, of which 2 were waited for; matrix products, arithmetic and copies ran while one was open for 0% of the time, Pallas kernels for 0%

profile of v2, /device:TPU:64, one launch (start us, length us, event | category | flops | bytes accessed | tf_op | source)
XLA Modules:
  0.0 457.6 jit_solution(3350081097873036498)
XLA Ops:
  7.2 0.0 all-reduce.5.cloned.1.call-start
  7.2 0.7 all-reduce.5.cloned.1.call-update
  7.9 0.0 all-gather.2.cloned.1.call-start
  7.9 0.7 all-gather.2.cloned.1.call-update
  8.6 62.2 %all-reduce.5.cloned.1.call-done = bf16[1024,512]{1,0:T(8,128)(2,1)} async-done(((bf16[1024,512]{1,0:T(8,128)(2,1)}), bf16[1024,512]{1,0:T(8,128)(2,1)}) %all-reduce.5.cloned.1.call-update) | async-done | bytes 1048592 | tf_op jit(solution)/shard_map/psum | solution.py:20
  70.8 1.7 fusion.5
  72.5 0.0 copy-start.8
  72.5 0.0 copy-start.5
  72.5 55.1 %all-gather.2.cloned.1.call-done = bf16[4,256,2048]{2,1,0:T(8,128)(2,1)} async-done(((bf16[1,256,2048]{2,1,0:T(8,128)(2,1)}), bf16[4,256,2048]{2,1,0:T(8,128)(2,1)}) %all-gather.2.cloned.1.call-update) | async-done | bytes 4194320 | tf_op jit(solution)/shard_map/all_gather | solution.py:19
  127.7 3.1 reduce_sum.66
  130.8 0.0 copy-start.7
  130.8 0.0 copy-start.6
  130.8 0.0 copy-start
  130.8 0.5 fusion.2
  131.3 16.8 %all-reduce.2 = (f32[256]{0:T(256)S(1)}, f32[1024]{0:T(1024)S(1)}) all-reduce(f32[256]{0:T(256)S(1)} %get-tuple-element.8, f32[1024]{0:T(1024)S(1)} %get-tuple-element.6), channel_id=1, replica_groups=mesh['dp'=4,'row'=16,'col'=8] {'col'}, use_global_device_ids=true, to_apply=%region_2.0 | all-reduce | flops 1280 | bytes 10240 | tf_op jit(solution)/shard_map/psum | solution.py:24
  148.1 0.0 copy-done.8
  148.1 0.0 copy-start.4
  148.1 45.7 %all-reduce.1 = (f32[2048]{0:T(1024)S(1)}, f32[512]{0:T(512)S(1)}) all-reduce(f32[2048]{0:T(1024)S(1)} %get-tuple-element.9, f32[512]{0:T(512)S(1)} %get-tuple-element.7), channel_id=1, replica_groups=mesh['dp'=4,'row'=16,'col'=8] {'row'}, use_global_device_ids=true, to_apply=%region_4.0 | all-reduce | flops 2560 | bytes 20480 | tf_op jit(solution)/shard_map/psum | solution.py:13
  193.8 0.0 copy-done.5
  193.8 0.0 copy-start.1
  193.8 1.5 multiply_reduce_fusion.1
  195.3 0.0 copy-done.7
  195.4 0.0 copy-start.3
  195.4 0.0 copy-done.6
  195.4 0.0 copy-done
  195.4 0.0 copy-start.2
  195.4 1.4 multiply_reduce_fusion
  196.8 249.7 %all-reduce = (f32[]{:T(128)}, f32[]{:T(128)}) all-reduce(f32[]{:T(128)} %multiply_reduce_fusion.1, f32[]{:T(128)} %multiply_reduce_fusion), channel_id=1, replica_groups=mesh['dp'=4,'row'=16,'col'=8] {'row','col'}, use_global_device_ids=true, to_apply=%region_6.0 | all-reduce | flops 2 | bytes 16 | tf_op jit(solution)/shard_map/psum | solution.py:35
  447.9 1.4 divide_convert_fusion.1
  449.4 0.0 copy-done.4
  449.4 0.0 copy-done.1
  449.4 1.4 divide_convert_fusion
  450.8 0.0 copy-done.3
  450.8 0.0 copy-done.2
  (4 shorter events, 0.0 us)
Async XLA Ops:
  7.2 63.7 %all-reduce.5.cloned.1.call-start = ((), (), s32[]{:S(2)}) async-start(), calls=%async_computation.1 | async-start | bytes 2097152 | tf_op jit(solution)/shard_map/psum | solution.py:20
  7.9 119.8 %all-gather.2.cloned.1.call-start = ((), (), s32[]{:S(2)}) async-start(), calls=%async_computation | async-start | bytes 5242880 | tf_op jit(solution)/shard_map/all_gather | solution.py:19
  72.5 75.5 %copy-start.8 = (f32[256]{0:T(256)S(1)}, f32[256]{0:T(256)}, u32[]{:S(2)}) copy-start(f32[256]{0:T(256)} %param.8) | copy-start | bytes 3076
  72.5 121.3 %copy-start.5 = (f32[2048]{0:T(1024)S(1)}, f32[2048]{0:T(1024)}, u32[]{:S(2)}) copy-start(f32[2048]{0:T(1024)} %param.9) | copy-start | bytes 24580
  130.8 64.6 %copy-start.7 = (f32[512]{0:T(512)S(1)}, f32[512]{0:T(512)}, u32[]{:S(2)}) copy-start(f32[512]{0:T(512)} %param.11) | copy-start | bytes 6148
  130.8 64.6 %copy-start.6 = (f32[1024]{0:T(1024)S(1)}, f32[1024]{0:T(1024)}, u32[]{:S(2)}) copy-start(f32[1024]{0:T(1024)} %param.10) | copy-start | bytes 12292
  130.8 64.6 %copy-start = (bf16[1024,512]{1,0:T(8,128)(2,1)S(1)}, bf16[1024,512]{1,0:T(8,128)(2,1)}, u32[]{:S(2)}) copy-start(bf16[1024,512]{1,0:T(8,128)(2,1)} %all-reduce.5.cloned.1.call-done) | copy-start | bytes 3145732
  148.1 301.3 %copy-start.4 = (f32[256]{0:T(256)}, f32[256]{0:T(256)S(1)}, u32[]{:S(2)}) copy-start(f32[256]{0:T(256)S(1)} %multiply_add_fusion.3) | copy-start | bytes 3076
  193.8 255.5 %copy-start.1 = (f32[2048]{0:T(1024)}, f32[2048]{0:T(1024)S(1)}, u32[]{:S(2)}) copy-start(f32[2048]{0:T(1024)S(1)} %multiply_add_fusion) | copy-start | bytes 24580
  195.4 255.4 %copy-start.3 = (f32[512]{0:T(512)}, f32[512]{0:T(512)S(1)}, u32[]{:S(2)}) copy-start(f32[512]{0:T(512)S(1)} %multiply_add_fusion.2) | copy-start | bytes 6148
  195.4 255.4 %copy-start.2 = (f32[1024]{0:T(1024)}, f32[1024]{0:T(1024)S(1)}, u32[]{:S(2)}) copy-start(f32[1024]{0:T(1024)S(1)} %multiply_add_fusion.1) | copy-start | bytes 12292
Sparse Core Ops, SparseCore 0:
  10.4 60.4 all-reduce.4
  73.1 54.4 all-gather.1
